TPU v7x, 128 devices: a whole 4x4x4 slice. The times are simulated.
128 devices in a mesh: space: 32 (over y, x, z_hi), shift: 4 (over z_lo, core).
Axes of the slice: x: 4, y: 4, z: 4 (z_hi: 2, z_lo: 2; z = z_hi * 2 + z_lo), core: 2. Of those that a mesh axis runs over, the one named last changes fastest.
Arguments:
- state: float32 [256, 256, 256], P('space'), may hold values from -13 to 13
- reaction: float32 [256, 256, 256], P('space'), may hold values from 0.05 to 0.5
Outputs:
- next_state: float32 [256, 256, 256], P(('space', 'shift'))
All inputs are finite; a program needn't handle non-finite values.
Results may differ from a plain program's by a relative error of at most 0.00017.
Values sent between devices are 32-bit elements; how exact they have to be, the bound alone decides.
A program may use at most 192 MiB of HBM per device.

v0:
```python
import math

import jax
import jax.numpy as jnp
from jax import lax
from jax.sharding import PartitionSpec as P

SH_DEV = 4
ITERS = 3


fraction = 0.4


def extended(block, sides, width):
    for axis, dim in sides:
        count = lax.axis_size(axis)
        forward = [(i, i + 1) for i in range(count - 1)]
        forward.append((count - 1, 0))
        backward = [(target, source) for source, target in forward]
        low = lax.ppermute(
            lax.slice_in_dim(block, block.shape[dim] - width, None, axis=dim), axis, forward
        )
        high = lax.ppermute(lax.slice_in_dim(block, 0, width, axis=dim), axis, backward)
        block = jnp.concatenate([low, block, high], axis=dim)
    return block


def operate(field, diagonal):
    padded = extended(field, (("space", 1),), 1)
    beside = padded[:, 2:] + padded[:, :-2]
    beside = beside + jnp.roll(field, 1, 2) + jnp.roll(field, -1, 2)
    beside = beside + jnp.roll(field, 1, 3) + jnp.roll(field, -1, 3)
    return diagonal * field - beside


def local_dots(left, right):
    return jnp.sum(left * right, axis=(1, 2, 3))


def squares(partial_value):
    return lax.psum(partial_value, "space")


def widen(values):
    return values[:, None, None, None]


def on_device(state, reaction):
    n_shift = lax.axis_size("shift")
    member = lax.axis_index("shift")
    shifts_all = SH_DEV * n_shift
    spacing = 10.0 / shifts_all
    coef = 2.0 * spacing * math.sin(math.pi * fraction) / math.pi
    node_index = jnp.arange(SH_DEV, dtype=jnp.int32) * n_shift + member
    nodes = spacing * (node_index.astype(jnp.float32) - shifts_all / 2 + 0.5)
    lifted = widen(jnp.exp(nodes))
    diagonal = lifted + 6.0 + reaction[None]
    stacked = jnp.broadcast_to(state[None], (SH_DEV,) + state.shape)
    first = operate(stacked, diagonal)
    solution = jnp.zeros_like(stacked)
    residual = stacked
    direction = stacked
    start = jnp.full((SH_DEV,), jnp.sum(state * state), jnp.float32)
    norm_now = squares(start)
    for step in range(ITERS):
        image = first if step == 0 else operate(direction, diagonal)
        alpha = norm_now / lax.psum(local_dots(direction, image), "space")
        solution = solution + widen(alpha) * direction
        residual = residual - widen(alpha) * image
        if step + 1 < ITERS:
            norm_next = squares(local_dots(residual, residual))
            direction = residual + widen(norm_next / norm_now) * direction
            norm_now = norm_next
    weights = coef * jnp.exp((1.0 - fraction) * nodes)
    local = jnp.sum(widen(weights) * solution, axis=0)
    whole = lax.psum(local, "shift")
    planes = local.shape[0] // n_shift
    return lax.dynamic_slice_in_dim(whole, member * planes, planes, 0)


def solution(mesh):
    in_specs = (P("space", None, None), P("space", None, None))
    out_specs = P(("space", "shift"), None, None)
    return jax.shard_map(
        on_device, mesh=mesh, in_specs=in_specs, out_specs=out_specs, check_vma=False
    )
```

profile of v0, /device:TPU:1, one launch (start us, length us, event | category | flops | bytes accessed | tf_op | source)
XLA Modules:
  0.0 791.8 jit_solution(647922646748788315)
XLA Ops:
  8.8 9.1 %collective-permute-start = (f32[4,1,256,256]{3,2,1,0:T(8,128)}, f32[4,1,256,256]{3,2,1,0:T(8,128)}, u32[]{:S(2)}, u32[]{:S(2)}) collective-permute-start(f32[4,1,256,256]{3,2,1,0:T(8,128)} %broadcast_in_dim.41), channel_id=1, source_target_pairs={{4,0},{8,4},{12,8},{16,12},{20,16},{24,20},{28,24},{32,28},{36,32}... | collective-permute-start | bytes 3145736 | tf_op jit(solution)/shard_map/ppermute | solution.py:24
  27.0 31.9 %collective-permute-done = f32[4,1,256,256]{3,2,1,0:T(8,128)} collective-permute-done((f32[4,1,256,256]{3,2,1,0:T(8,128)}, f32[4,1,256,256]{3,2,1,0:T(8,128)}, u32[]{:S(2)}, u32[]{:S(2)}) %collective-permute-start) | collective-permute-done | bytes 1048608 | tf_op jit(solution)/shard_map/ppermute | solution.py:24
  83.9 25.1 %multiply_reduce_fusion.4 = (f32[4]{0:T(128)S(1)}, f32[4,8,256,256]{3,2,1,0:T(8,128)}) fusion(f32[8,256,256]{2,1,0:T(8,128)S(1)} %copy-done.1, f32[4,8,256,1]{3,2,1,0:T(8,128)} %broadcast_in_dim.50, f32[4,8,256,255]{3,2,1,0:T(8,128)} %broadcast_in_dim.49, f32[4,8,256,255]{3,2,1,0:T(8,128)} %broadcast_in_dim.48, f32[4,8,256,1]{3,2,1,0:T(8,128)S(1)} %broadcast_in_dim.47, ...), kind=kLoop, calls=%fused_computation.37 | loop fusion | flops 33554428 | bytes 56623136 | tf_op jit(solution)/shard_map/reduce_sum | solution.py:38
  109.6 82.8 %all-reduce = (f32[4]{0:T(128)S(1)}, f32[4]{0:T(128)S(1)}) all-reduce(f32[4]{0:T(128)S(1)} %broadcast_in_dim.39, f32[4]{0:T(128)S(1)} %get-tuple-element.9), channel_id=1, replica_groups=mesh['space'=32,'shift'=4] {'space'}, use_global_device_ids=true, to_apply=%region_1.2 | all-reduce | flops 8 | bytes 64 | tf_op jit(solution)/shard_map/psum | solution.py:42
  192.4 4.9 multiply_reduce_fusion.3
  197.3 75.1 %psum.51 = f32[4]{0:T(128)S(1)} all-reduce(f32[4]{0:T(128)S(1)} %multiply_reduce_fusion.3), channel_id=1, replica_groups=mesh['space'=32,'shift'=4] {'space'}, use_global_device_ids=true, to_apply=%region_5.6 | all-reduce | flops 4 | bytes 32 | tf_op jit(solution)/shard_map/psum | solution.py:42
  272.4 5.0 multiply_add_fusion.1
  277.4 6.6 fusion.29
  284.0 4.8 fusion.30
  292.3 7.3 fusion.31
  299.6 16.0 %collective-permute-done.2 = f32[4,1,256,256]{3,2,1,0:T(8,128)} collective-permute-done((f32[4,1,256,256]{3,2,1,0:T(8,128)S(1)}, f32[4,1,256,256]{3,2,1,0:T(8,128)}, u32[]{:S(2)}, u32[]{:S(2)}) %collective-permute-start.2) | collective-permute-done | bytes 1048608 | tf_op jit(solution)/shard_map/ppermute | solution.py:24
  315.6 18.7 %multiply_reduce_fusion.2 = (f32[4]{0:T(128)S(1)}, f32[4,8,256,256]{3,2,1,0:T(8,128)}) fusion(f32[4,8,256,256]{3,2,1,0:T(8,128)S(1)} %multiply_add_fusion.1, f32[4,8,256,1]{3,2,1,0:T(8,128)} %get-tuple-element.28, f32[4,8,256,255]{3,2,1,0:T(8,128)} %get-tuple-element.30, f32[4,8,256,255]{3,2,1,0:T(8,128)} %get-tuple-element.29, ...), kind=kLoop, calls=%fused_computation.33 | loop fusion | flops 33554428 | bytes 54525984 | tf_op jit(solution)/shard_map/reduce_sum | solution.py:38
  334.3 81.0 %psum.52 = f32[4]{0:T(128)S(1)} all-reduce(f32[4]{0:T(128)S(1)} %get-tuple-element.7), channel_id=1, replica_groups=mesh['space'=32,'shift'=4] {'space'}, use_global_device_ids=true, to_apply=%region_7.8 | all-reduce | flops 4 | bytes 32 | tf_op jit(solution)/shard_map/psum | solution.py:68
  415.3 6.9 multiply_reduce_fusion.1
  422.2 75.1 %psum.53 = f32[4]{0:T(128)S(1)} all-reduce(f32[4]{0:T(128)S(1)} %multiply_reduce_fusion.1), channel_id=1, replica_groups=mesh['space'=32,'shift'=4] {'space'}, use_global_device_ids=true, to_apply=%region_9.10 | all-reduce | flops 4 | bytes 32 | tf_op jit(solution)/shard_map/psum | solution.py:42
  497.3 7.0 multiply_add_fusion
  504.4 7.7 fusion.22
  512.1 4.8 fusion.23
  520.4 6.6 fusion.24
  527.0 16.9 %collective-permute-done.4 = f32[4,1,256,256]{3,2,1,0:T(8,128)S(1)} collective-permute-done((f32[4,1,256,256]{3,2,1,0:T(8,128)S(1)}, f32[4,1,256,256]{3,2,1,0:T(8,128)S(1)}, u32[]{:S(2)}, u32[]{:S(2)}) %collective-permute-start.4) | collective-permute-done | bytes 1048608 | tf_op jit(solution)/shard_map/ppermute | solution.py:24
  543.9 15.8 %fusion.4 = f32[4]{0:T(128)S(1)} fusion(f32[4,8,256,256]{3,2,1,0:T(8,128)S(1)} %multiply_add_fusion, f32[4,1,256,256]{3,2,1,0:T(8,128)} %collective-permute-done.5, f32[4,1,256,256]{3,2,1,0:T(8,128)S(1)} %collective-permute-done.4, f32[4,8,255,256]{3,2,1,0:T(8,128)} %get-tuple-element.16, f32[4,8,1,256]{3,2,1,0:T(1,128)S(1)} %get-tuple-element.18, ...), kind=kLoop, calls=%fused_computation.7 | loop fusion | flops 33554428 | bytes 46137376 | tf_op jit(solution)/shard_map/reduce_sum | solution.py:38
  559.7 88.3 %psum.54 = f32[4]{0:T(128)S(1)} all-reduce(f32[4]{0:T(128)S(1)} %fusion.4), channel_id=1, replica_groups=mesh['space'=32,'shift'=4] {'space'}, use_global_device_ids=true, to_apply=%region_11.12 | all-reduce | flops 4 | bytes 32 | tf_op jit(solution)/shard_map/psum | solution.py:68
  648.0 9.0 %multiply_reduce_fusion = f32[8,256,256]{2,1,0:T(8,128)} fusion(f32[4,8,256,256]{3,2,1,0:T(8,128)} %copy-done, f32[4]{0:T(128)S(1)} %div.19, f32[4]{0:T(128)S(1)} %div.17, f32[4]{0:T(128)S(1)} %div.15, f32[8,256,256]{2,1,0:T(8,128)S(1)} %copy-done.1, f32[4]{0:T(128)S(1)} %exponential_multiply_fusion, f32[4]{0:T(128)S(1)} %div.16, ...), kind=kLoop, calls=%fused_computation.29 | loop fusion | flops 22544384 | bytes 20971600 | tf_op jit(solution)/shard_map/reduce_sum | solution.py:76
  657.0 126.0 %all-reduce.3.cloned.1.call-done = f32[8,256,256]{2,1,0:T(8,128)} async-done(((f32[8,256,256]{2,1,0:T(8,128)}), f32[8,256,256]{2,1,0:T(8,128)}) %all-reduce.3.cloned.1.call-update) | async-done | bytes 2097168 | tf_op jit(solution)/shard_map/psum | solution.py:77
  (53 shorter events, 45.9 us)
Async XLA Ops:
  6.5 16.3 %copy-start.1 = (f32[8,256,256]{2,1,0:T(8,128)S(1)}, f32[8,256,256]{2,1,0:T(8,128)}, u32[]{:S(2)}) copy-start(f32[8,256,256]{2,1,0:T(8,128)} %param.2) | copy-start | bytes 6291460
  6.5 776.5 %all-reduce.3.cloned.1.call-start = ((), (), s32[]{:S(2)}) async-start(), calls=%async_computation | async-start | bytes 4194304 | tf_op jit(solution)/shard_map/psum | solution.py:77
  8.8 50.1 %collective-permute-start = (f32[4,1,256,256]{3,2,1,0:T(8,128)}, f32[4,1,256,256]{3,2,1,0:T(8,128)}, u32[]{:S(2)}, u32[]{:S(2)}) collective-permute-start(f32[4,1,256,256]{3,2,1,0:T(8,128)} %broadcast_in_dim.41), channel_id=1, source_target_pairs={{4,0},{8,4},{12,8},{16,12},{20,16},{24,20},{28,24},{32,28},{36,32}... | collective-permute-start | bytes 3145736 | tf_op jit(solution)/shard_map/ppermute | solution.py:24
  19.0 40.8 %collective-permute-start.1 = (f32[4,1,256,256]{3,2,1,0:T(8,128)}, f32[4,1,256,256]{3,2,1,0:T(8,128)}, u32[]{:S(2)}, u32[]{:S(2)}) collective-permute-start(f32[4,1,256,256]{3,2,1,0:T(8,128)} %broadcast_in_dim.42), channel_id=1, source_target_pairs={{0,4},{4,8},{8,12},{12,16},{16,20},{20,24},{24,28},{28,32},{32,36}... | collective-permute-start | bytes 3145736 | tf_op jit(solution)/shard_map/ppermute | solution.py:21
  77.0 6.9 copy-start.2
  288.9 26.7 %collective-permute-start.2 = (f32[4,1,256,256]{3,2,1,0:T(8,128)S(1)}, f32[4,1,256,256]{3,2,1,0:T(8,128)}, u32[]{:S(2)}, u32[]{:S(2)}) collective-permute-start(f32[4,1,256,256]{3,2,1,0:T(8,128)S(1)} %get-tuple-element.21), channel_id=1, source_target_pairs={{4,0},{8,4},{12,8},{16,12},{20,16},{24,20},{28,24},{32,28},{36,32}... | collective-permute-start | bytes 3145736 | tf_op jit(solution)/shard_map/ppermute | solution.py:24
  292.2 23.4 %collective-permute-start.3 = (f32[4,1,256,256]{3,2,1,0:T(8,128)S(1)}, f32[4,1,256,256]{3,2,1,0:T(8,128)}, u32[]{:S(2)}, u32[]{:S(2)}) collective-permute-start(f32[4,1,256,256]{3,2,1,0:T(8,128)S(1)} %get-tuple-element.22), channel_id=1, source_target_pairs={{0,4},{4,8},{8,12},{12,16},{16,20},{20,24},{24,28},{28,32},{32,36}... | collective-permute-start | bytes 3145736 | tf_op jit(solution)/shard_map/ppermute | solution.py:21
  292.3 23.3 %copy-start.3 = (f32[8,256,256]{2,1,0:T(8,128)S(1)}, f32[8,256,256]{2,1,0:T(8,128)}, u32[]{:S(2)}) copy-start(f32[8,256,256]{2,1,0:T(8,128)} %param.3) | copy-start | bytes 6291460
  504.4 39.5 %copy-start = (f32[4,8,256,256]{3,2,1,0:T(8,128)}, f32[4,8,256,256]{3,2,1,0:T(8,128)S(1)}, u32[]{:S(2)}) copy-start(f32[4,8,256,256]{3,2,1,0:T(8,128)S(1)} %multiply_add_fusion) | copy-start | bytes 25165828
  517.1 26.8 %collective-permute-start.4 = (f32[4,1,256,256]{3,2,1,0:T(8,128)S(1)}, f32[4,1,256,256]{3,2,1,0:T(8,128)S(1)}, u32[]{:S(2)}, u32[]{:S(2)}) collective-permute-start(f32[4,1,256,256]{3,2,1,0:T(8,128)S(1)} %get-tuple-element.19), channel_id=1, source_target_pairs={{4,0},{8,4},{12,8},{16,12},{20,16},{24,20},{28,24},{32,28},{36,32}... | collective-permute-start | bytes 3145736 | tf_op jit(solution)/shard_map/ppermute | solution.py:24
  520.4 23.5 %collective-permute-start.5 = (f32[4,1,256,256]{3,2,1,0:T(8,128)S(1)}, f32[4,1,256,256]{3,2,1,0:T(8,128)}, u32[]{:S(2)}, u32[]{:S(2)}) collective-permute-start(f32[4,1,256,256]{3,2,1,0:T(8,128)S(1)} %get-tuple-element.20), channel_id=1, source_target_pairs={{0,4},{4,8},{8,12},{12,16},{16,20},{20,24},{24,28},{28,32},{32,36}... | collective-permute-start | bytes 3145736 | tf_op jit(solution)/shard_map/ppermute | solution.py:21
  520.4 23.4 %copy-start.4 = (f32[8,256,256]{2,1,0:T(8,128)S(1)}, f32[8,256,256]{2,1,0:T(8,128)}, u32[]{:S(2)}) copy-start(f32[8,256,256]{2,1,0:T(8,128)} %param.3) | copy-start | bytes 6291460
Sparse Core Ops, SparseCore 0:
  657.2 125.8 all-reduce.2
where the time goes:
time: 792 us
  blocking collectives  402 us (51%)
  waiting for transfers between devices  192 us (24%)
  other arithmetic  93.6 us (12%)
  local copies, waits for them, and re-layouts  74.9 us (9%)
  starting transfers between devices  15.7 us (2%)
  between operations  13.6 us (2%)
    psum x3, blocking collectives, squares(): return lax.psum(partial_value, 'space')  233 us
    psum x2, blocking collectives, on_device(): alpha = norm_now / lax.psum(local_dots(direction, image), 'space')  169 us
    psum x1, waiting for transfers between devices, on_device(): whole = lax.psum(local, 'shift')  126 us
    reduce_sum x5, other arithmetic, local_dots(): return jnp.sum(left * right, axis=(1, 2, 3))  71.4 us
    ppermute x3, waiting for transfers between devices, extended(): lax.ppermute(lax.slice_in_dim(block, 0, width, axis=dim), axis, backward)  64.8 us
    slice x6, local copies, waits for them, and re-layouts, operate(): beside = beside + jnp.roll(field, 1, 3) + jnp.roll(field, -1, 3)  28.2 us
    broadcast_in_dim x11, local copies, waits for them, and re-layouts, on_device(): stacked = jnp.broadcast_to(state[None], (SH_DEV,) + state.shape)  26.2 us
  transfers between devices with their start and end apart: 7, of which 5 were waited for; matrix products, arithmetic and copies ran while one was open for 3% of the time, Pallas kernels for 0%

commit v1 on v0

v1 whole, which is shorter than its diff:
```python
import functools
import math

import jax
import jax.numpy as jnp
from jax import lax
from jax.experimental import pallas as pl
from jax.experimental.pallas import tpu as pltpu
from jax.sharding import PartitionSpec as P

MESH = pl.DeviceIdType.MESH
SH_DEV = 4
FRACTION = 0.4
LOW, HIGH = 0.05, 12.5
PIECES = 4
PAD = 8


def two_sum(a, b):
    s = a + b
    t = s - a
    return s, (a - (s - t)) + (b - t)


def quick(s, e):
    t = s + e
    return t, e - (t - s)


def split(a):
    c = a * 4097.0
    h = c - (c - a)
    return h, a - h


def mul(a, b):
    p = a[0] * b[0]
    ah, al = split(a[0])
    bh, bl = split(b[0])
    e = ((ah * bh - p) + ah * bl + al * bh) + al * bl
    return quick(p, e + (a[0] * b[1] + a[1] * b[0]))


def add(a, b):
    s, e = two_sum(a[0], b[0])
    return quick(s, e + (a[1] + b[1]))


def neg(a):
    return -a[0], -a[1]


def sub(a, b):
    return add(a, neg(b))


def div(a, b):
    q = a[0] / b[0]
    r = sub(a, mul((q, jnp.zeros_like(q)), b))
    return quick(q, r[0] / b[0])


def clamp(a):
    inside = (a[0] >= LOW) & (a[0] <= HIGH)
    edge = jnp.where(a[0] < LOW, LOW, HIGH)
    return jnp.where(inside, a[0], edge), jnp.where(inside, a[1], 0.0)


def nonneg(a):
    keep = a[0] > 0.0
    return jnp.where(keep, a[0], 0.0), jnp.where(keep, a[1], 0.0)


def coefficients(m, shifts_all):
    one = jnp.ones_like(m[0][0])
    a0 = clamp(div(m[1], m[0]))
    g1 = nonneg(sub(m[2], mul(a0, m[1])))
    h1 = add(sub(m[3], mul((2.0 * a0[0], 2.0 * a0[1]), m[2])), mul(mul(a0, a0), m[1]))
    some1 = g1[0] > 0.0
    g1s = jnp.where(some1, g1[0], one), jnp.where(some1, g1[1], 0.0)
    a1 = clamp(div(h1, g1s))
    b1 = nonneg(div(g1, m[0]))
    s = neg(add(a0, a1))
    t = sub(mul(a0, a1), b1)
    r3 = add(m[4], add(mul(s, m[3]), mul(t, m[2])))
    g2 = nonneg(r3)
    h2 = add(add(m[5], mul(s, m[4])), add(mul(t, m[3]), mul(s, r3)))
    some2 = g2[0] > 0.0
    g2s = jnp.where(some2, g2[0], one)
    a0, a1, b1, t, s = a0[0], a1[0], b1[0], t[0], s[0]
    a2 = jnp.clip(h2[0] / g2s, LOW, HIGH)
    b1 = jnp.minimum(b1, jnp.maximum((HIGH - a0) * (a0 - LOW), 0.0))
    b2 = jnp.minimum(g2[0] / g1s[0], jnp.maximum((HIGH - a1) * (a1 - LOW), 0.0))

    lane = lax.broadcasted_iota(jnp.int32, one.shape, 1)
    spacing = 10.0 / shifts_all
    coef = 2.0 * spacing * math.sin(math.pi * FRACTION) / math.pi
    node = spacing * (jnp.minimum(lane, shifts_all - 1).astype(jnp.float32) - shifts_all / 2 + 0.5)
    weight = jnp.where(lane < shifts_all, coef * jnp.exp((1.0 - FRACTION) * node), 0.0)
    sigma = jnp.exp(node)
    d2 = sigma + a2
    d1 = jnp.maximum((sigma + a1) - b2 / d2, sigma + LOW)
    d0 = jnp.maximum((sigma + a0) - b1 / d1, sigma + LOW)
    y0 = weight / d0
    y1 = -y0 / d1
    y2 = -y1 / d2
    y0, y1, y2 = (jnp.sum(y, axis=1, keepdims=True) for y in (y0, y1, y2))
    a0, s, t = a0[:, :1], s[:, :1], t[:, :1]
    return y0 - a0 * y1 + t * y2, y1 + s * y2, y2


def kernel(
    n_space, n_shift, column, state, reaction, out,
    bb, rr, v1, v2, w0, recv_b, recv_v, recv_w, acc, tile, tiles, pair, pairs,
    load_b, load_r, send_x, got_b, got_v, got_w, send_1, got_1, send_2, got_2,
):
    space, member = lax.axis_index("space"), lax.axis_index("shift")
    planes, rows, width = state.shape
    piece = rows // PIECES
    half = n_shift // 2
    high = member // half
    is_outer = (member % (n_shift - 1)) == 0
    outer = jnp.where(is_outer, 1, 0)
    depth = 2 * (1 - outer)

    def plane(k):
        return k + high * (planes - 1 - 2 * k)

    step = 2 * high - 1
    partner = (lax.rem(space + step + n_space, n_space), (n_shift - 1) * (1 - high))
    deep = column // n_shift
    here = lax.rem(space, deep) * n_shift + member
    column_at = space // deep
    columns = n_space // deep

    def beside(k):
        other = lax.rem(here + k, column)
        return column_at * deep + other // n_shift, lax.rem(other, n_shift)

    def across(k):
        return lax.rem(column_at + k, columns) * deep + lax.rem(space, deep), member

    barrier = pltpu.get_barrier_semaphore()

    @pl.when(is_outer)
    def _():
        pl.semaphore_signal(barrier, inc=1, device_id=partner, device_id_type=MESH)

    for k in range(1, column):
        pl.semaphore_signal(barrier, inc=1, device_id=beside(k), device_id_type=MESH)
    for k in range(1, columns):
        pl.semaphore_signal(barrier, inc=1, device_id=across(k), device_id_type=MESH)

    def get_b(j):
        return pltpu.make_async_copy(
            state.at[plane(depth - 2 + j)], bb.at[j, pl.ds(PAD, rows)], load_b.at[j])

    def get_r(j):
        return pltpu.make_async_copy(reaction.at[plane(depth - 1 + j)], rr.at[j], load_r.at[j])

    @pl.when(is_outer)
    def _():
        for j in range(2, 7):
            get_b(j).start()
        for j in range(1, 5):
            get_r(j).start()

    @pl.when(jnp.logical_not(is_outer))
    def _():
        for j in range(7):
            get_b(j).start()
        for j in range(5):
            get_r(j).start()

    acc[...] = jnp.zeros_like(acc)
    tile[...] = jnp.zeros_like(tile)
    pl.semaphore_wait(barrier, column + columns - 2 + outer)

    def wrap(ref, j):
        ref[j, PAD - 1 : PAD] = ref[j, PAD + rows - 1 : PAD + rows]
        ref[j, PAD + rows : PAD + rows + 1] = ref[j, PAD : PAD + 1]

    def at(ref, j, c, shift=0):
        return ref[j, pl.ds(PAD + c * piece + shift, piece)]

    def rows_of(c, start=0):
        first = c * piece + start
        return pl.ds(first if isinstance(c, int) else pl.multiple_of(first, 8), piece)

    def put(ref, j, c, value):
        ref[j, rows_of(c, PAD)] = value

    def coef_at(j, c):
        return rr[j, rows_of(c)] + 6.0

    def flat(ref, j, c):
        return ref[j, rows_of(c, PAD)]

    def applied(ref, j, c, r, sides):
        x = flat(ref, j, c)
        near = at(ref, j, c, -1) + at(ref, j, c, 1)
        near = near + pltpu.roll(x, 1, 1) + pltpu.roll(x, width - 1, 1)
        for side in sides:
            near = near + flat(ref, side, c)
        return coef_at(r, c) * x - near

    def gather(k, product):
        acc[k] += jnp.sum(product.reshape(piece // 8, 8, width), axis=0)

    def each(body):
        for c in range(PIECES):
            body(c)

    def make_v1(j, sides):
        each(lambda c: put(v1, j, c, applied(bb, j + 1, c, j, sides)))
        wrap(v1, j)

    def make_v2(k, sides):
        each(lambda c: put(v2, k, c, applied(v1, k + 1, c, k + 1, sides)))

    def early(j):
        def body(c):
            b, v = flat(bb, j, c), flat(v1, j - 1, c)
            gather(0, b * b)
            gather(1, b * v)
            gather(2, v * v)

        each(body)

    def late(k):
        def body(c):
            v, u = flat(v1, k + 1, c), flat(v2, k, c)
            gather(3, v * u)
            gather(4, u * u)

        each(body)

    def last(k, scale):
        def body(c):
            u = flat(v2, k, c)
            near = pltpu.roll(u, width - 1, 1) + at(v2, k, c, 1)
            near = near + scale * flat(v2, k + 1, c)
            gather(5, u * (coef_at(k + 1, c) * u - 2.0 * near))

        each(body)

    @pl.when(jnp.logical_not(is_outer))
    def _():
        for j in range(7):
            get_b(j).wait()
        for j in range(1, 6):
            wrap(bb, j)
        for j in range(5):
            get_r(j).wait()
        for j in range(5):
            make_v1(j, (j, j + 2))
        for k in range(3):
            make_v2(k, (k, k + 2))
        for k in range(2):
            wrap(v2, k)
            early(k + 2)
            late(k)
        last(0, 1.0)
        last(1, 0.5)

    @pl.when(is_outer)
    def _():
        def send_b(c):
            return pltpu.make_async_remote_copy(
                src_ref=state.at[plane(0), pl.ds(c * piece, piece)], dst_ref=recv_b.at[c],
                send_sem=send_x.at[c], recv_sem=got_b.at[c],
                device_id=partner, device_id_type=MESH)

        def send_v(c):
            return pltpu.make_async_remote_copy(
                src_ref=v1.at[1, pl.ds(PAD + c * piece, piece)], dst_ref=recv_v.at[c],
                send_sem=send_x.at[PIECES + c], recv_sem=got_v.at[c],
                device_id=partner, device_id_type=MESH)

        def send_w(i):
            return pltpu.make_async_remote_copy(
                src_ref=w0.at[2 * i + high], dst_ref=recv_w.at[i],
                send_sem=send_x.at[2 * PIECES + i], recv_sem=got_w.at[i],
                device_id=partner, device_id_type=MESH)

        for c in range(PIECES):
            send_b(c).start()
        for j in range(2, 7):
            get_b(j).wait()
        for j in range(2, 6):
            wrap(bb, j)
        for j in range(1, 5):
            get_r(j).wait()
        make_v1(1, (3,))
        for j in range(2, 5):
            make_v1(j, (j, j + 2))
        make_v2(2, (2, 4))
        make_v2(1, (3,))
        early(3)
        for c in range(PIECES):
            send_b(c).wait_recv()
            b = flat(bb, 2, c)
            v = flat(v1, 1, c) - recv_b[c]
            put(v1, 1, c, v)
            send_v(c).start()
            gather(0, b * b)
            gather(1, b * v)
            gather(2, v * v)
        wrap(v1, 1)

        def own_w(c):
            w0[c] = applied(v1, 1, c, 1, (2,))

        for i in range(PIECES // 2):
            own_w(2 * i)
            own_w(2 * i + 1)
            send_w(i).start()
        each(lambda c: put(v2, 1, c, flat(v2, 1, c) - flat(v1, 1, c)))
        wrap(v2, 1)
        late(1)
        last(1, 1.0)
        for c in range(PIECES):
            send_v(c).wait_recv()
            u = w0[c] - recv_v[c]
            put(v2, 0, c, u)
            gather(3, flat(v1, 1, c) * u)
            gather(4, u * u)
        wrap(v2, 0)
        last(0, 1.0)
        for i in range(PIECES // 2):
            c = 2 * i + 1 - high
            send_w(i).wait_recv()
            gather(5, -2.0 * flat(v2, 0, c) * (recv_w[i] - flat(v1, 1, c)))
        for c in range(PIECES):
            send_b(c).wait_send()
            send_v(c).wait_send()
        for i in range(PIECES // 2):
            send_w(i).wait_send()

    for k in range(6):
        row = acc[k]
        row = row[:, : width // 2] + row[:, width // 2 :]
        tile[k : k + 1] = jnp.sum(row, axis=0, keepdims=True)

    def step_1(k):
        return pltpu.make_async_remote_copy(
            src_ref=tile, dst_ref=tiles.at[k], send_sem=send_1.at[k], recv_sem=got_1.at[k],
            device_id=beside(k), device_id_type=MESH)

    def step_2(k):
        return pltpu.make_async_remote_copy(
            src_ref=pair, dst_ref=pairs.at[k], send_sem=send_2.at[k], recv_sem=got_2.at[k],
            device_id=across(k), device_id_type=MESH)

    for k in range(1, column):
        step_1(k).start()
    hi, lo = tile[...], jnp.zeros(tile.shape, jnp.float32)
    for k in range(1, column):
        step_1(k).wait_recv()
        hi, e = two_sum(hi, tiles[k])
        lo = lo + e
    pair[0] = hi
    pair[1] = lo
    for k in range(1, columns):
        step_2(k).start()
    for k in range(1, columns):
        step_2(k).wait_recv()
        hi, e = two_sum(hi, pairs[k, 0])
        lo = lo + (e + pairs[k, 1])
    turn = hi.shape[1] // 2
    while turn:
        hi, e = two_sum(hi, pltpu.roll(hi, turn, 1))
        lo = (lo + pltpu.roll(lo, turn, 1)) + e
        turn //= 2
    hi, lo = quick(hi, lo)
    moments = [(hi[k : k + 1], lo[k : k + 1]) for k in range(6)]
    c0, c1, c2 = coefficients(moments, SH_DEV * n_shift)

    for k in range(2):
        def body(c, k=k):
            value = c0 * flat(bb, k + 2, c) + c1 * flat(v1, k + 1, c) + c2 * flat(v2, k, c)
            out[k + high * (1 - 2 * k), rows_of(c)] = value

        each(body)
    for k in range(1, column):
        step_1(k).wait_send()
    for k in range(1, columns):
        step_2(k).wait_send()


def on_device(state, reaction):
    n_space, n_shift = lax.axis_size("space"), lax.axis_size("shift")
    planes, rows, width = state.shape
    column = 2 * n_shift
    columns = n_space * n_shift // column
    piece = rows // PIECES
    f32 = jnp.float32
    padded = rows + 2 * PAD
    dma = pltpu.SemaphoreType.DMA
    cells = 2 * rows * width
    return pl.pallas_call(
        functools.partial(kernel, n_space, n_shift, column),
        out_shape=jax.ShapeDtypeStruct((planes // n_shift, rows, width), f32),
        in_specs=[pl.BlockSpec(memory_space=pl.ANY)] * 2,
        out_specs=pl.BlockSpec(memory_space=pltpu.VMEM),
        scratch_shapes=[
            pltpu.VMEM((7, padded, width), f32),
            pltpu.VMEM((5, rows, width), f32),
            pltpu.VMEM((5, padded, width), f32),
            pltpu.VMEM((3, padded, width), f32),
            pltpu.VMEM((PIECES, piece, width), f32),
            pltpu.VMEM((PIECES, piece, width), f32),
            pltpu.VMEM((PIECES, piece, width), f32),
            pltpu.VMEM((PIECES // 2, piece, width), f32),
            pltpu.VMEM((6, 8, width), f32),
            pltpu.VMEM((8, width // 2), f32),
            pltpu.VMEM((column, 8, width // 2), f32),
            pltpu.VMEM((2, 8, width // 2), f32),
            pltpu.VMEM((columns, 2, 8, width // 2), f32),
            dma((7,)),
            dma((5,)),
            dma((2 * PIECES + PIECES // 2,)),
            dma((PIECES,)),
            dma((PIECES,)),
            dma((PIECES // 2,)),
            dma((column,)),
            dma((column,)),
            dma((columns,)),
            dma((columns,)),
        ],
        compiler_params=pltpu.CompilerParams(
            collective_id=0, has_side_effects=True, vmem_limit_bytes=60 * 2**20),
        cost_estimate=pl.CostEstimate(
            flops=100 * cells, bytes_accessed=40 * cells, transcendentals=0),
    )(state, reaction)


def solution(mesh):
    in_specs = (P("space", None, None), P("space", None, None))
    out_specs = P(("space", "shift"), None, None)
    return jax.shard_map(
        on_device, mesh=mesh, in_specs=in_specs, out_specs=out_specs, check_vma=False
    )
```

time: 792 us -> 33.5 us (0.04)
  blocking collectives: 402 us -> 0 us
  waiting for transfers between devices: 192 us -> 0 us
  other arithmetic: 93.6 us -> 0 us
  local copies, waits for them, and re-layouts: 74.9 us -> 1.87 us
  Pallas kernels: 0 us -> 31.5 us
  starting transfers between devices: 15.7 us -> 0 us
  between operations: 13.6 us -> 0.01 us
    psum x5 -> x0, blocking collectives: 402 us -> none  [the longest x3 233 us: squares(): return lax.psum(partial_value, 'space')]
    psum x1 -> x0, waiting for transfers between devices: 126 us -> none  [on_device(): whole = lax.psum(local, 'shift')]
    reduce_sum x7 -> x0, other arithmetic: 81.5 us -> none  [the longest x5 71.4 us: local_dots(): return jnp.sum(left * right, axis=(1, 2, 3))]
    ppermute x6 -> x0, waiting for transfers between devices: 65.7 us -> none  [the longest x3 64.8 us: extended(): lax.ppermute(lax.slice_in_dim(block, 0, width, axis=dim), axis, backward)]
    slice x16 -> x0, local copies, waits for them, and re-layouts: 44.3 us -> none  [the longest x6 28.2 us: operate(): beside = beside + jnp.roll(field, 1, 3) + jnp.roll(field, -1, 3)]
    pallas_call x0 -> x1, Pallas kernels: none -> 31.5 us  [on_device(): pl.pallas_call(functools.partial(kernel, n_space, n_shift, column), out_s...]
    broadcast_in_dim x12 -> x0, local copies, waits for them, and re-layouts: 26.9 us -> none  [the longest x11 26.2 us: on_device(): stacked = jnp.broadcast_to(state[None], (SH_DEV,) + state.shape)]
    ppermute x6 -> x0, starting transfers between devices: 15.7 us -> none  [the longest x3 15.7 us: extended(): lax.ppermute(lax.slice_in_dim(block, 0, width, axis=dim), axis, backward)]
  transfers between devices with their start and end apart: 7 -> 0, of which waited for: 5 -> 0; matrix products, arithmetic and copies ran while one was open for 3% -> 0% of each run, Pallas kernels for 0% -> 0%
where the time goes in v1:
time: 33.5 us; the launch traced here: 33.4 us
  Pallas kernels  31.5 us (94%)
  local copies, waits for them, and re-layouts  1.87 us (6%)
    pallas_call x1, Pallas kernels, on_device(): pl.pallas_call(functools.partial(kernel, n_space, n_shift, column), out_s...  31.5 us
    unnamed x1, local copies, waits for them, and re-layouts  1.87 us

profile of v1, /device:TPU:1, one launch (start us, length us, event | category | flops | bytes accessed | tf_op | source)
XLA Modules:
  0.0 33.4 jit_solution(816554029771352207)
XLA Ops:
  0.0 31.5 %shard_map.28 = f32[2,256,256]{2,1,0:T(8,128)} custom-call(f32[8,256,256]{2,1,0:T(8,128)} %state.1, f32[8,256,256]{2,1,0:T(8,128)} %reaction.1), custom_call_target="tpu_custom_call" | custom-call | flops 13107200 | bytes 5242880 | tf_op jit(solution)/shard_map/pallas_call | solution.py:401
  31.5 1.9 %copy.4 = f32[2,256,256]{2,1,0:T(8,128)} copy(f32[2,256,256]{2,1,0:T(8,128)} %shard_map.28) | data formatting | bytes 1048576

commit v2 on v1

--- a/solution.py
+++ b/solution.py
@@ -400,8 +400,8 @@
     cells = 2 * rows * width
     return pl.pallas_call(
         functools.partial(kernel, n_space, n_shift, column),
-        out_shape=jax.ShapeDtypeStruct((planes // n_shift, rows, width), f32),
-        in_specs=[pl.BlockSpec(memory_space=pl.ANY)] * 2,
+        out_shape=pltpu.VMEM((planes // n_shift, rows, width), f32),
+        in_specs=[pl.BlockSpec(memory_space=pltpu.HBM)] * 2,
         out_specs=pl.BlockSpec(memory_space=pltpu.VMEM),
         scratch_shapes=[
             pltpu.VMEM((7, padded, width), f32),
@@ -429,7 +429,7 @@
             dma((columns,)),
         ],
         compiler_params=pltpu.CompilerParams(
-            collective_id=0, has_side_effects=True, vmem_limit_bytes=60 * 2**20),
+            collective_id=0, has_side_effects=True, vmem_limit_bytes=58 * 2**20),
         cost_estimate=pl.CostEstimate(
             flops=100 * cells, bytes_accessed=40 * cells, transcendentals=0),
     )(state, reaction)

time: 33.5 us -> 31.6 us (0.943)
  local copies, waits for them, and re-layouts: 1.87 us -> 0.8 us
  Pallas kernels: 31.5 us -> 30.7 us
    unnamed x1, local copies, waits for them, and re-layouts: 1.87 us -> 0.8 us
    pallas_call x1, Pallas kernels: 31.5 us -> 30.7 us  [on_device(): pl.pallas_call(functools.partial(kernel, n_space, n_shift, column), out_s...]
where the time goes in v2:
time: 31.6 us; the launch traced here: 31.5 us
  Pallas kernels  30.7 us (97%)
  local copies, waits for them, and re-layouts  0.8 us (3%)
    pallas_call x1, Pallas kernels, on_device(): pl.pallas_call(functools.partial(kernel, n_space, n_shift, column), out_s...  30.7 us
    unnamed x1, local copies, waits for them, and re-layouts  0.8 us

profile of v2, /device:TPU:1, one launch (start us, length us, event | category | flops | bytes accessed | tf_op | source)
XLA Modules:
  0.0 31.5 jit_solution(13231924631033431033)
XLA Ops:
  0.0 30.7 %shard_map.28 = f32[2,256,256]{2,1,0:T(8,128)S(1)} custom-call(f32[8,256,256]{2,1,0:T(8,128)} %state.1, f32[8,256,256]{2,1,0:T(8,128)} %reaction.1), custom_call_target="tpu_custom_call" | custom-call | flops 13107200 | bytes 5242880 | tf_op jit(solution)/shard_map/pallas_call | solution.py:401
  30.7 0.8 %copy.4 = f32[2,256,256]{2,1,0:T(8,128)} copy(f32[2,256,256]{2,1,0:T(8,128)S(1)} %shard_map.28) | data formatting | bytes 1048576

commit v3 on v2

--- a/solution.py
+++ b/solution.py
@@ -111,8 +111,8 @@
 
 def kernel(
     n_space, n_shift, column, state, reaction, out,
-    bb, rr, v1, v2, w0, recv_b, recv_v, recv_w, acc, tile, tiles, pair, pairs,
-    load_b, load_r, send_x, got_b, got_v, got_w, send_1, got_1, send_2, got_2,
+    bb, rr, v1, v2, u0, w0, p0, recv_b, recv_u, recv_p, recv_r, acc, tile, tiles, pair, pairs,
+    load_b, load_r, send_x, got_b, got_u, got_p, got_r, send_1, got_1, send_2, got_2,
 ):
     space, member = lax.axis_index("space"), lax.axis_index("shift")
     planes, rows, width = state.shape
@@ -173,7 +173,6 @@
             get_r(j).start()
 
     acc[...] = jnp.zeros_like(acc)
-    tile[...] = jnp.zeros_like(tile)
     pl.semaphore_wait(barrier, column + columns - 2 + outer)
 
     def wrap(ref, j):
@@ -271,28 +270,61 @@
                 send_sem=send_x.at[c], recv_sem=got_b.at[c],
                 device_id=partner, device_id_type=MESH)
 
-        def send_v(c):
+        def send_u(c):
             return pltpu.make_async_remote_copy(
-                src_ref=v1.at[1, pl.ds(PAD + c * piece, piece)], dst_ref=recv_v.at[c],
-                send_sem=send_x.at[PIECES + c], recv_sem=got_v.at[c],
+                src_ref=u0.at[0, pl.ds(PAD + c * piece, piece)], dst_ref=recv_u.at[c],
+                send_sem=send_x.at[PIECES + c], recv_sem=got_u.at[c],
                 device_id=partner, device_id_type=MESH)
 
-        def send_w(i):
+        def send_p(c):
             return pltpu.make_async_remote_copy(
-                src_ref=w0.at[2 * i + high], dst_ref=recv_w.at[i],
-                send_sem=send_x.at[2 * PIECES + i], recv_sem=got_w.at[i],
+                src_ref=p0.at[c], dst_ref=recv_p.at[c],
+                send_sem=send_x.at[2 * PIECES + c], recv_sem=got_p.at[c],
                 device_id=partner, device_id_type=MESH)
+
+        def send_r(c):
+            return pltpu.make_async_remote_copy(
+                src_ref=reaction.at[plane(0), pl.ds(c * piece, piece)], dst_ref=recv_r.at[c],
+                send_sem=send_x.at[3 * PIECES + c], recv_sem=got_r.at[c],
+                device_id=partner, device_id_type=MESH)
+
+        late_half = lax.rem(space, 2) == 1
+        early_half = jnp.logical_not(late_half)
+        from_late, from_early = range(PIECES - 1), range(PIECES - 1, PIECES)
 
         for c in range(PIECES):
             send_b(c).start()
         for j in range(2, 7):
             get_b(j).wait()
-        for j in range(2, 6):
-            wrap(bb, j)
+        wrap(bb, 2)
         for j in range(1, 5):
             get_r(j).wait()
-        make_v1(1, (3,))
-        for j in range(2, 5):
+        for c in range(PIECES):
+            put(u0, 0, c, applied(bb, 2, c, 1, (3,)))
+            send_u(c).start()
+        wrap(u0, 0)
+        for j in range(3, 6):
+            wrap(bb, j)
+        make_v1(2, (2, 4))
+
+        def own_p(c):
+            p0[c] = applied(u0, 0, c, 1, ()) - flat(v1, 2, c)
+
+        @pl.when(late_half)
+        def _():
+            for c in from_late:
+                own_p(c)
+                send_p(c).start()
+                send_r(c).start()
+
+        @pl.when(early_half)
+        def _():
+            for c in from_early:
+                own_p(c)
+                send_p(c).start()
+                send_r(c).start()
+
+        for j in range(3, 5):
             make_v1(j, (j, j + 2))
         make_v2(2, (2, 4))
         make_v2(1, (3,))
@@ -300,47 +332,81 @@
         for c in range(PIECES):
             send_b(c).wait_recv()
             b = flat(bb, 2, c)
-            v = flat(v1, 1, c) - recv_b[c]
+            v = flat(u0, 0, c) - recv_b[c]
             put(v1, 1, c, v)
-            send_v(c).start()
             gather(0, b * b)
             gather(1, b * v)
             gather(2, v * v)
         wrap(v1, 1)
-
-        def own_w(c):
+        for c in range(PIECES):
             w0[c] = applied(v1, 1, c, 1, (2,))
-
-        for i in range(PIECES // 2):
-            own_w(2 * i)
-            own_w(2 * i + 1)
-            send_w(i).start()
         each(lambda c: put(v2, 1, c, flat(v2, 1, c) - flat(v1, 1, c)))
         wrap(v2, 1)
         late(1)
         last(1, 1.0)
         for c in range(PIECES):
-            send_v(c).wait_recv()
-            u = w0[c] - recv_v[c]
+            send_u(c).wait_recv()
+            u = w0[c] - (recv_u[c] - flat(bb, 2, c))
             put(v2, 0, c, u)
             gather(3, flat(v1, 1, c) * u)
             gather(4, u * u)
         wrap(v2, 0)
         last(0, 1.0)
-        for i in range(PIECES // 2):
-            c = 2 * i + 1 - high
-            send_w(i).wait_recv()
-            gather(5, -2.0 * flat(v2, 0, c) * (recv_w[i] - flat(v1, 1, c)))
+
+        def edge(c):
+            send_p(c).wait_recv()
+            send_r(c).wait_recv()
+            b = flat(bb, 2, c)
+            near = at(bb, 2, c, -1) + at(bb, 2, c, 1)
+            near = near + pltpu.roll(b, 1, 1) + pltpu.roll(b, width - 1, 1)
+            far = recv_p[c] - ((recv_r[c] + 6.0) * b - near) - flat(v1, 1, c)
+            gather(5, -2.0 * flat(v2, 0, c) * far)
+
+        @pl.when(early_half)
+        def _():
+            for c in from_late:
+                edge(c)
+
+        @pl.when(late_half)
+        def _():
+            for c in from_early:
+                edge(c)
+
         for c in range(PIECES):
             send_b(c).wait_send()
-            send_v(c).wait_send()
-        for i in range(PIECES // 2):
-            send_w(i).wait_send()
-
+            send_u(c).wait_send()
+
+        @pl.when(late_half)
+        def _():
+            for c in from_late:
+                send_p(c).wait_send()
+                send_r(c).wait_send()
+
+        @pl.when(early_half)
+        def _():
+            for c in from_early:
+                send_p(c).wait_send()
+                send_r(c).wait_send()
+
+    lanes = width // 2
+    hi = jnp.zeros((8, lanes), jnp.float32)
+    lane = lax.broadcasted_iota(jnp.int32, hi.shape, 1)
+    line = lax.broadcasted_iota(jnp.int32, hi.shape, 0)
     for k in range(6):
         row = acc[k]
-        row = row[:, : width // 2] + row[:, width // 2 :]
-        tile[k : k + 1] = jnp.sum(row, axis=0, keepdims=True)
+        row = jnp.sum(row[:, :lanes] + row[:, lanes:], axis=0, keepdims=True)
+        hi = jnp.where(line == k, row, hi)
+    lo = jnp.zeros_like(hi)
+    turn = lanes // 2
+    while turn:
+        hi, e = two_sum(hi, pltpu.roll(hi, turn, 1))
+        lo = (lo + pltpu.roll(lo, turn, 1)) + e
+        turn //= 2
+    packed = jnp.where(lane == line, hi, 0.0) + jnp.where(lane == line + 8, lo, 0.0)
+    tile[...] = jnp.sum(packed, axis=0, keepdims=True)
+
+    def merge(total, lost):
+        return total + jnp.where(lane[:1] >= 8, pltpu.roll(lost, 8, 1), 0.0)
 
     def step_1(k):
         return pltpu.make_async_remote_copy(
@@ -354,24 +420,23 @@
 
     for k in range(1, column):
         step_1(k).start()
-    hi, lo = tile[...], jnp.zeros(tile.shape, jnp.float32)
+    total, lost = tile[...], jnp.zeros(tile.shape, jnp.float32)
     for k in range(1, column):
         step_1(k).wait_recv()
-        hi, e = two_sum(hi, tiles[k])
-        lo = lo + e
-    pair[0] = hi
-    pair[1] = lo
+        total, e = two_sum(total, tiles[k])
+        lost = lost + e
+    pair[...] = merge(total, lost)
     for k in range(1, columns):
         step_2(k).start()
+    total, lost = pair[...], jnp.zeros(tile.shape, jnp.float32)
     for k in range(1, columns):
         step_2(k).wait_recv()
-        hi, e = two_sum(hi, pairs[k, 0])
-        lo = lo + (e + pairs[k, 1])
-    turn = hi.shape[1] // 2
-    while turn:
-        hi, e = two_sum(hi, pltpu.roll(hi, turn, 1))
-        lo = (lo + pltpu.roll(lo, turn, 1)) + e
-        turn //= 2
+        total, e = two_sum(total, pairs[k])
+        lost = lost + e
+    total = jnp.broadcast_to(merge(total, lost), hi.shape)
+    hi = jnp.sum(jnp.where(lane == line, total, 0.0), axis=1, keepdims=True)
+    lo = jnp.sum(jnp.where(lane == line + 8, total, 0.0), axis=1, keepdims=True)
+    hi, lo = jnp.broadcast_to(hi, lane.shape), jnp.broadcast_to(lo, lane.shape)
     hi, lo = quick(hi, lo)
     moments = [(hi[k : k + 1], lo[k : k + 1]) for k in range(6)]
     c0, c1, c2 = coefficients(moments, SH_DEV * n_shift)
@@ -408,21 +473,25 @@
             pltpu.VMEM((5, rows, width), f32),
             pltpu.VMEM((5, padded, width), f32),
             pltpu.VMEM((3, padded, width), f32),
+            pltpu.VMEM((1, padded, width), f32),
             pltpu.VMEM((PIECES, piece, width), f32),
             pltpu.VMEM((PIECES, piece, width), f32),
             pltpu.VMEM((PIECES, piece, width), f32),
-            pltpu.VMEM((PIECES // 2, piece, width), f32),
+            pltpu.VMEM((PIECES, piece, width), f32),
+            pltpu.VMEM((PIECES, piece, width), f32),
+            pltpu.VMEM((PIECES, piece, width), f32),
             pltpu.VMEM((6, 8, width), f32),
-            pltpu.VMEM((8, width // 2), f32),
-            pltpu.VMEM((column, 8, width // 2), f32),
-            pltpu.VMEM((2, 8, width // 2), f32),
-            pltpu.VMEM((columns, 2, 8, width // 2), f32),
+            pltpu.VMEM((1, width // 2), f32),
+            pltpu.VMEM((column, 1, width // 2), f32),
+            pltpu.VMEM((1, width // 2), f32),
+            pltpu.VMEM((columns, 1, width // 2), f32),
             dma((7,)),
             dma((5,)),
-            dma((2 * PIECES + PIECES // 2,)),
+            dma((4 * PIECES,)),
             dma((PIECES,)),
             dma((PIECES,)),
-            dma((PIECES // 2,)),
+            dma((PIECES,)),
+            dma((PIECES,)),
             dma((column,)),
             dma((column,)),
             dma((columns,)),

time: 31.6 us -> 30.3 us (0.959)
  Pallas kernels: 30.7 us -> 29.3 us
    pallas_call x1, Pallas kernels: 30.7 us -> 29.3 us  [on_device(): pl.pallas_call(functools.partial(kernel, n_space, n_shift, column), out_s...]
where the time goes in v3:
time: 30.3 us; the launch traced here: 30.1 us
  Pallas kernels  29.3 us (97%)
  local copies, waits for them, and re-layouts  0.8 us (3%)
    pallas_call x1, Pallas kernels, on_device(): pl.pallas_call(functools.partial(kernel, n_space, n_shift, column), out_s...  29.3 us
    unnamed x1, local copies, waits for them, and re-layouts  0.8 us

profile of v3, /device:TPU:1, one launch (start us, length us, event | category | flops | bytes accessed | tf_op | source)
XLA Modules:
  0.0 30.1 jit_solution(12355047158213438147)
XLA Ops:
  0.0 29.3 %shard_map.28 = f32[2,256,256]{2,1,0:T(8,128)S(1)} custom-call(f32[8,256,256]{2,1,0:T(8,128)} %state.1, f32[8,256,256]{2,1,0:T(8,128)} %reaction.1), custom_call_target="tpu_custom_call" | custom-call | flops 13107200 | bytes 5242880 | tf_op jit(solution)/shard_map/pallas_call | solution.py:466
  29.3 0.8 %copy.4 = f32[2,256,256]{2,1,0:T(8,128)} copy(f32[2,256,256]{2,1,0:T(8,128)S(1)} %shard_map.28) | data formatting | bytes 1048576

commit v4 on v3

--- a/solution.py
+++ b/solution.py
@@ -129,16 +129,30 @@
     step = 2 * high - 1
     partner = (lax.rem(space + step + n_space, n_space), (n_shift - 1) * (1 - high))
     deep = column // n_shift
-    here = lax.rem(space, deep) * n_shift + member
-    column_at = space // deep
-    columns = n_space // deep
+    chips = column // 2
+    side = math.isqrt(n_space // deep)
+    z, core = lax.rem(space, deep) * half + high, lax.rem(member, 2)
+    y, x = space // deep // side, lax.rem(space // deep, side)
+
+    def hops(distance, size):
+        return min(distance, size - distance)
+
+    up = sorted(
+        ((dz, dc) for dz in range(chips) for dc in range(2) if dz + dc),
+        key=lambda d: (-hops(d[0], chips), d))
+    wide = sorted(
+        ((dy, dx) for dy in range(side) for dx in range(side) if dy + dx),
+        key=lambda d: (-hops(d[0], side) - hops(d[1], side), d))
 
     def beside(k):
-        other = lax.rem(here + k, column)
-        return column_at * deep + other // n_shift, lax.rem(other, n_shift)
+        dz, dc = up[k]
+        z2 = lax.rem(z + dz, chips)
+        return space - lax.rem(space, deep) + z2 // half, lax.rem(z2, half) * 2 + lax.rem(core + dc, 2)
 
     def across(k):
-        return lax.rem(column_at + k, columns) * deep + lax.rem(space, deep), member
+        dy, dx = wide[k]
+        chip = lax.rem(y + dy, side) * side + lax.rem(x + dx, side)
+        return chip * deep + lax.rem(space, deep), member
 
     barrier = pltpu.get_barrier_semaphore()
 
@@ -146,10 +160,11 @@
     def _():
         pl.semaphore_signal(barrier, inc=1, device_id=partner, device_id_type=MESH)
 
-    for k in range(1, column):
+    for k in range(len(wide)):
+        pl.semaphore_signal(barrier, inc=1, device_id=across(k), device_id_type=MESH)
+    for k in range(len(up)):
         pl.semaphore_signal(barrier, inc=1, device_id=beside(k), device_id_type=MESH)
-    for k in range(1, columns):
-        pl.semaphore_signal(barrier, inc=1, device_id=across(k), device_id_type=MESH)
+    pl.semaphore_wait(barrier, len(up) + len(wide) + outer)
 
     def get_b(j):
         return pltpu.make_async_copy(
@@ -158,22 +173,7 @@
     def get_r(j):
         return pltpu.make_async_copy(reaction.at[plane(depth - 1 + j)], rr.at[j], load_r.at[j])
 
-    @pl.when(is_outer)
-    def _():
-        for j in range(2, 7):
-            get_b(j).start()
-        for j in range(1, 5):
-            get_r(j).start()
-
-    @pl.when(jnp.logical_not(is_outer))
-    def _():
-        for j in range(7):
-            get_b(j).start()
-        for j in range(5):
-            get_r(j).start()
-
     acc[...] = jnp.zeros_like(acc)
-    pl.semaphore_wait(barrier, column + columns - 2 + outer)
 
     def wrap(ref, j):
         ref[j, PAD - 1 : PAD] = ref[j, PAD + rows - 1 : PAD + rows]
@@ -245,6 +245,10 @@
 
     @pl.when(jnp.logical_not(is_outer))
     def _():
+        for j in range(7):
+            get_b(j).start()
+        for j in range(5):
+            get_r(j).start()
         for j in range(7):
             get_b(j).wait()
         for j in range(1, 6):
@@ -295,6 +299,10 @@
         for c in range(PIECES):
             send_b(c).start()
         for j in range(2, 7):
+            get_b(j).start()
+        for j in range(1, 5):
+            get_r(j).start()
+        for j in range(2, 7):
             get_b(j).wait()
         wrap(bb, 2)
         for j in range(1, 5):
@@ -408,32 +416,32 @@
     def merge(total, lost):
         return total + jnp.where(lane[:1] >= 8, pltpu.roll(lost, 8, 1), 0.0)
 
-    def step_1(k):
+    def row_to(source, rows, k, send, got, to):
         return pltpu.make_async_remote_copy(
-            src_ref=tile, dst_ref=tiles.at[k], send_sem=send_1.at[k], recv_sem=got_1.at[k],
-            device_id=beside(k), device_id_type=MESH)
-
-    def step_2(k):
+            src_ref=source, dst_ref=rows.at[k], send_sem=send, recv_sem=got,
+            device_id=to, device_id_type=MESH)
+
+    def all_rows(rows, send, got):
         return pltpu.make_async_remote_copy(
-            src_ref=pair, dst_ref=pairs.at[k], send_sem=send_2.at[k], recv_sem=got_2.at[k],
-            device_id=across(k), device_id_type=MESH)
-
-    for k in range(1, column):
-        step_1(k).start()
-    total, lost = tile[...], jnp.zeros(tile.shape, jnp.float32)
-    for k in range(1, column):
-        step_1(k).wait_recv()
-        total, e = two_sum(total, tiles[k])
-        lost = lost + e
-    pair[...] = merge(total, lost)
-    for k in range(1, columns):
-        step_2(k).start()
-    total, lost = pair[...], jnp.zeros(tile.shape, jnp.float32)
-    for k in range(1, columns):
-        step_2(k).wait_recv()
-        total, e = two_sum(total, pairs[k])
-        lost = lost + e
-    total = jnp.broadcast_to(merge(total, lost), hi.shape)
+            src_ref=rows, dst_ref=rows, send_sem=send, recv_sem=got,
+            device_id=across(0), device_id_type=MESH)
+
+    def summed(own, rows):
+        total, lost = own, jnp.zeros(own.shape, jnp.float32)
+        for k in range(rows.shape[0]):
+            total, e = two_sum(total, rows[k])
+            lost = lost + e
+        return merge(total, lost)
+
+    for k in range(len(up)):
+        row_to(tile, tiles, k, send_1, got_1, beside(k)).start()
+    all_rows(tiles, send_1, got_1).wait_recv()
+    pair[...] = summed(tile[...], tiles)
+    for k in range(len(wide)):
+        row_to(pair, pairs, k, send_2, got_2, across(k)).start()
+    all_rows(pairs, send_2, got_2).wait_recv()
+    total = summed(pair[...], pairs)
+    total = jnp.broadcast_to(total, hi.shape)
     hi = jnp.sum(jnp.where(lane == line, total, 0.0), axis=1, keepdims=True)
     lo = jnp.sum(jnp.where(lane == line + 8, total, 0.0), axis=1, keepdims=True)
     hi, lo = jnp.broadcast_to(hi, lane.shape), jnp.broadcast_to(lo, lane.shape)
@@ -447,10 +455,8 @@
             out[k + high * (1 - 2 * k), rows_of(c)] = value
 
         each(body)
-    for k in range(1, column):
-        step_1(k).wait_send()
-    for k in range(1, columns):
-        step_2(k).wait_send()
+    all_rows(tiles, send_1, got_1).wait_send()
+    all_rows(pairs, send_2, got_2).wait_send()
 
 
 def on_device(state, reaction):
@@ -482,9 +488,9 @@
             pltpu.VMEM((PIECES, piece, width), f32),
             pltpu.VMEM((6, 8, width), f32),
             pltpu.VMEM((1, width // 2), f32),
-            pltpu.VMEM((column, 1, width // 2), f32),
+            pltpu.VMEM((column - 1, 1, width // 2), f32),
             pltpu.VMEM((1, width // 2), f32),
-            pltpu.VMEM((columns, 1, width // 2), f32),
+            pltpu.VMEM((columns - 1, 1, width // 2), f32),
             dma((7,)),
             dma((5,)),
             dma((4 * PIECES,)),
@@ -492,10 +498,10 @@
             dma((PIECES,)),
             dma((PIECES,)),
             dma((PIECES,)),
-            dma((column,)),
-            dma((column,)),
-            dma((columns,)),
-            dma((columns,)),
+            dma,
+            dma,
+            dma,
+            dma,
         ],
         compiler_params=pltpu.CompilerParams(
             collective_id=0, has_side_effects=True, vmem_limit_bytes=58 * 2**20),

time: 30.3 us -> 29.8 us (0.983)
  Pallas kernels: 29.3 us -> 28.8 us
    pallas_call x1, Pallas kernels: 29.3 us -> 28.8 us  [on_device(): pl.pallas_call(functools.partial(kernel, n_space, n_shift, column), out_s...]
where the time goes in v4:
time: 29.8 us; the launch traced here: 29.6 us
  Pallas kernels  28.8 us (97%)
  local copies, waits for them, and re-layouts  0.8 us (3%)
    pallas_call x1, Pallas kernels, on_device(): pl.pallas_call(functools.partial(kernel, n_space, n_shift, column), out_s...  28.8 us
    unnamed x1, local copies, waits for them, and re-layouts  0.8 us

profile of v4, /device:TPU:1, one launch (start us, length us, event | category | flops | bytes accessed | tf_op | source)
XLA Modules:
  0.0 29.6 jit_solution(1709631352614588634)
XLA Ops:
  0.0 28.8 %shard_map.28 = f32[2,256,256]{2,1,0:T(8,128)S(1)} custom-call(f32[8,256,256]{2,1,0:T(8,128)} %state.1, f32[8,256,256]{2,1,0:T(8,128)} %reaction.1), custom_call_target="tpu_custom_call" | custom-call | flops 13107200 | bytes 5242880 | tf_op jit(solution)/shard_map/pallas_call | solution.py:472
  28.8 0.8 %copy.4 = f32[2,256,256]{2,1,0:T(8,128)} copy(f32[2,256,256]{2,1,0:T(8,128)S(1)} %shard_map.28) | data formatting | bytes 1048576

commit v5 on v4

--- a/solution.py
+++ b/solution.py
@@ -71,7 +71,17 @@
     return jnp.where(keep, a[0], 0.0), jnp.where(keep, a[1], 0.0)
 
 
-def coefficients(m, shifts_all):
+def quadrature(shifts_all, shape):
+    lane = lax.broadcasted_iota(jnp.int32, shape, 1)
+    spacing = 10.0 / shifts_all
+    coef = 2.0 * spacing * math.sin(math.pi * FRACTION) / math.pi
+    node = spacing * (jnp.minimum(lane, shifts_all - 1).astype(jnp.float32) - shifts_all / 2 + 0.5)
+    weight = jnp.where(lane < shifts_all, coef * jnp.exp((1.0 - FRACTION) * node), 0.0)
+    sigma = jnp.exp(node)
+    return sigma, weight
+
+
+def coefficients(m, sigma, weight):
     one = jnp.ones_like(m[0][0])
     a0 = clamp(div(m[1], m[0]))
     g1 = nonneg(sub(m[2], mul(a0, m[1])))
@@ -92,12 +102,6 @@
     b1 = jnp.minimum(b1, jnp.maximum((HIGH - a0) * (a0 - LOW), 0.0))
     b2 = jnp.minimum(g2[0] / g1s[0], jnp.maximum((HIGH - a1) * (a1 - LOW), 0.0))
 
-    lane = lax.broadcasted_iota(jnp.int32, one.shape, 1)
-    spacing = 10.0 / shifts_all
-    coef = 2.0 * spacing * math.sin(math.pi * FRACTION) / math.pi
-    node = spacing * (jnp.minimum(lane, shifts_all - 1).astype(jnp.float32) - shifts_all / 2 + 0.5)
-    weight = jnp.where(lane < shifts_all, coef * jnp.exp((1.0 - FRACTION) * node), 0.0)
-    sigma = jnp.exp(node)
     d2 = sigma + a2
     d1 = jnp.maximum((sigma + a1) - b2 / d2, sigma + LOW)
     d0 = jnp.maximum((sigma + a0) - b1 / d1, sigma + LOW)
@@ -164,7 +168,6 @@
         pl.semaphore_signal(barrier, inc=1, device_id=across(k), device_id_type=MESH)
     for k in range(len(up)):
         pl.semaphore_signal(barrier, inc=1, device_id=beside(k), device_id_type=MESH)
-    pl.semaphore_wait(barrier, len(up) + len(wide) + outer)
 
     def get_b(j):
         return pltpu.make_async_copy(
@@ -173,7 +176,74 @@
     def get_r(j):
         return pltpu.make_async_copy(reaction.at[plane(depth - 1 + j)], rr.at[j], load_r.at[j])
 
+    def send_b(c, source=None):
+        if source is None:
+            source = state.at[plane(0), pl.ds(c * piece, piece)]
+        return pltpu.make_async_remote_copy(
+            src_ref=source, dst_ref=recv_b.at[c],
+            send_sem=send_x.at[c], recv_sem=got_b.at[c],
+            device_id=partner, device_id_type=MESH)
+
+    def send_u(c):
+        return pltpu.make_async_remote_copy(
+            src_ref=u0.at[0, pl.ds(PAD + c * piece, piece)], dst_ref=recv_u.at[c],
+            send_sem=send_x.at[PIECES + c], recv_sem=got_u.at[c],
+            device_id=partner, device_id_type=MESH)
+
+    def send_p(c):
+        return pltpu.make_async_remote_copy(
+            src_ref=p0.at[c], dst_ref=recv_p.at[c],
+            send_sem=send_x.at[2 * PIECES + c], recv_sem=got_p.at[c],
+            device_id=partner, device_id_type=MESH)
+
+    def send_r(c):
+        return pltpu.make_async_remote_copy(
+            src_ref=reaction.at[plane(0), pl.ds(c * piece, piece)], dst_ref=recv_r.at[c],
+            send_sem=send_x.at[3 * PIECES + c], recv_sem=got_r.at[c],
+            device_id=partner, device_id_type=MESH)
+
+    late_half = lax.rem(space, 2) == 1
+    early_half = jnp.logical_not(late_half)
+    from_late, from_early = range(PIECES - 1), range(PIECES - 1, PIECES)
+
+    def loads():
+        @pl.when(is_outer)
+        def _():
+            for j in range(2, 7):
+                get_b(j).start()
+            for j in range(1, 5):
+                get_r(j).start()
+
+        @pl.when(jnp.logical_not(is_outer))
+        def _():
+            for j in range(7):
+                get_b(j).start()
+            for j in range(5):
+                get_r(j).start()
+
     acc[...] = jnp.zeros_like(acc)
+
+    @pl.when(early_half)
+    def _():
+        loads()
+        get_b(2).wait()
+
+    pl.semaphore_wait(barrier, len(up) + len(wide) + outer)
+
+    @pl.when(is_outer & early_half)
+    def _():
+        for c in range(PIECES):
+            send_b(c, bb.at[2, pl.ds(PAD + c * piece, piece)]).start()
+
+    @pl.when(late_half)
+    def _():
+        @pl.when(is_outer)
+        def _():
+            for c in range(PIECES):
+                send_b(c).start()
+
+        loads()
+        get_b(2).wait()
 
     def wrap(ref, j):
         ref[j, PAD - 1 : PAD] = ref[j, PAD + rows - 1 : PAD + rows]
@@ -245,11 +315,7 @@
 
     @pl.when(jnp.logical_not(is_outer))
     def _():
-        for j in range(7):
-            get_b(j).start()
-        for j in range(5):
-            get_r(j).start()
-        for j in range(7):
+        for j in (0, 1, 3, 4, 5, 6):
             get_b(j).wait()
         for j in range(1, 6):
             wrap(bb, j)
@@ -268,41 +334,7 @@
 
     @pl.when(is_outer)
     def _():
-        def send_b(c):
-            return pltpu.make_async_remote_copy(
-                src_ref=state.at[plane(0), pl.ds(c * piece, piece)], dst_ref=recv_b.at[c],
-                send_sem=send_x.at[c], recv_sem=got_b.at[c],
-                device_id=partner, device_id_type=MESH)
-
-        def send_u(c):
-            return pltpu.make_async_remote_copy(
-                src_ref=u0.at[0, pl.ds(PAD + c * piece, piece)], dst_ref=recv_u.at[c],
-                send_sem=send_x.at[PIECES + c], recv_sem=got_u.at[c],
-                device_id=partner, device_id_type=MESH)
-
-        def send_p(c):
-            return pltpu.make_async_remote_copy(
-                src_ref=p0.at[c], dst_ref=recv_p.at[c],
-                send_sem=send_x.at[2 * PIECES + c], recv_sem=got_p.at[c],
-                device_id=partner, device_id_type=MESH)
-
-        def send_r(c):
-            return pltpu.make_async_remote_copy(
-                src_ref=reaction.at[plane(0), pl.ds(c * piece, piece)], dst_ref=recv_r.at[c],
-                send_sem=send_x.at[3 * PIECES + c], recv_sem=got_r.at[c],
-                device_id=partner, device_id_type=MESH)
-
-        late_half = lax.rem(space, 2) == 1
-        early_half = jnp.logical_not(late_half)
-        from_late, from_early = range(PIECES - 1), range(PIECES - 1, PIECES)
-
-        for c in range(PIECES):
-            send_b(c).start()
-        for j in range(2, 7):
-            get_b(j).start()
-        for j in range(1, 5):
-            get_r(j).start()
-        for j in range(2, 7):
+        for j in range(3, 7):
             get_b(j).wait()
         wrap(bb, 2)
         for j in range(1, 5):
@@ -380,22 +412,6 @@
             for c in from_early:
                 edge(c)
 
-        for c in range(PIECES):
-            send_b(c).wait_send()
-            send_u(c).wait_send()
-
-        @pl.when(late_half)
-        def _():
-            for c in from_late:
-                send_p(c).wait_send()
-                send_r(c).wait_send()
-
-        @pl.when(early_half)
-        def _():
-            for c in from_early:
-                send_p(c).wait_send()
-                send_r(c).wait_send()
-
     lanes = width // 2
     hi = jnp.zeros((8, lanes), jnp.float32)
     lane = lax.broadcasted_iota(jnp.int32, hi.shape, 1)
@@ -404,12 +420,10 @@
         row = acc[k]
         row = jnp.sum(row[:, :lanes] + row[:, lanes:], axis=0, keepdims=True)
         hi = jnp.where(line == k, row, hi)
-    lo = jnp.zeros_like(hi)
-    turn = lanes // 2
-    while turn:
-        hi, e = two_sum(hi, pltpu.roll(hi, turn, 1))
-        lo = (lo + pltpu.roll(lo, turn, 1)) + e
-        turn //= 2
+    grid = 192.0 * jnp.max(jnp.abs(hi), axis=1, keepdims=True)
+    coarse = (hi + grid) - grid
+    hi, lo = two_sum(
+        jnp.sum(coarse, axis=1, keepdims=True), jnp.sum(hi - coarse, axis=1, keepdims=True))
     packed = jnp.where(lane == line, hi, 0.0) + jnp.where(lane == line + 8, lo, 0.0)
     tile[...] = jnp.sum(packed, axis=0, keepdims=True)
 
@@ -439,15 +453,36 @@
     pair[...] = summed(tile[...], tiles)
     for k in range(len(wide)):
         row_to(pair, pairs, k, send_2, got_2, across(k)).start()
+    all_rows(tiles, send_1, got_1).wait_send()
+
+    @pl.when(is_outer)
+    def _():
+        for c in range(PIECES):
+            send_b(c).wait_send()
+            send_u(c).wait_send()
+
+        @pl.when(late_half)
+        def _():
+            for c in from_late:
+                send_p(c).wait_send()
+                send_r(c).wait_send()
+
+        @pl.when(early_half)
+        def _():
+            for c in from_early:
+                send_p(c).wait_send()
+                send_r(c).wait_send()
+
+    sigma, weight = quadrature(SH_DEV * n_shift, tile.shape)
     all_rows(pairs, send_2, got_2).wait_recv()
     total = summed(pair[...], pairs)
-    total = jnp.broadcast_to(total, hi.shape)
+    total = jnp.broadcast_to(total, lane.shape)
     hi = jnp.sum(jnp.where(lane == line, total, 0.0), axis=1, keepdims=True)
     lo = jnp.sum(jnp.where(lane == line + 8, total, 0.0), axis=1, keepdims=True)
     hi, lo = jnp.broadcast_to(hi, lane.shape), jnp.broadcast_to(lo, lane.shape)
     hi, lo = quick(hi, lo)
     moments = [(hi[k : k + 1], lo[k : k + 1]) for k in range(6)]
-    c0, c1, c2 = coefficients(moments, SH_DEV * n_shift)
+    c0, c1, c2 = coefficients(moments, sigma, weight)
 
     for k in range(2):
         def body(c, k=k):
@@ -455,7 +490,6 @@
             out[k + high * (1 - 2 * k), rows_of(c)] = value
 
         each(body)
-    all_rows(tiles, send_1, got_1).wait_send()
     all_rows(pairs, send_2, got_2).wait_send()
 
 

time: 29.8 us -> 29.2 us (0.980)
  Pallas kernels: 28.8 us -> 28.2 us
    pallas_call x1, Pallas kernels: 28.8 us -> 28.2 us  [on_device(): pl.pallas_call(functools.partial(kernel, n_space, n_shift, column), out_s...]
where the time goes in v5:
time: 29.2 us; the launch traced here: 29 us
  Pallas kernels  28.2 us (97%)
  local copies, waits for them, and re-layouts  0.8 us (3%)
    pallas_call x1, Pallas kernels, on_device(): pl.pallas_call(functools.partial(kernel, n_space, n_shift, column), out_s...  28.2 us
    unnamed x1, local copies, waits for them, and re-layouts  0.8 us

profile of v5, /device:TPU:1, one launch (start us, length us, event | category | flops | bytes accessed | tf_op | source)
XLA Modules:
  0.0 29.0 jit_solution(9691572761443095608)
XLA Ops:
  0.0 28.2 %shard_map.28 = f32[2,256,256]{2,1,0:T(8,128)S(1)} custom-call(f32[8,256,256]{2,1,0:T(8,128)} %state.1, f32[8,256,256]{2,1,0:T(8,128)} %reaction.1), custom_call_target="tpu_custom_call" | custom-call | flops 13107200 | bytes 5242880 | tf_op jit(solution)/shard_map/pallas_call | solution.py:506
  28.2 0.8 %copy.4 = f32[2,256,256]{2,1,0:T(8,128)} copy(f32[2,256,256]{2,1,0:T(8,128)S(1)} %shard_map.28) | data formatting | bytes 1048576

commit v6 on v5

--- a/solution.py
+++ b/solution.py
@@ -196,6 +196,12 @@
             send_sem=send_x.at[2 * PIECES + c], recv_sem=got_p.at[c],
             device_id=partner, device_id_type=MESH)
 
+    def send_w(c):
+        return pltpu.make_async_remote_copy(
+            src_ref=w0.at[c], dst_ref=recv_p.at[c],
+            send_sem=send_x.at[2 * PIECES + c], recv_sem=got_p.at[c],
+            device_id=partner, device_id_type=MESH)
+
     def send_r(c):
         return pltpu.make_async_remote_copy(
             src_ref=reaction.at[plane(0), pl.ds(c * piece, piece)], dst_ref=recv_r.at[c],
@@ -357,13 +363,6 @@
                 send_p(c).start()
                 send_r(c).start()
 
-        @pl.when(early_half)
-        def _():
-            for c in from_early:
-                own_p(c)
-                send_p(c).start()
-                send_r(c).start()
-
         for j in range(3, 5):
             make_v1(j, (j, j + 2))
         make_v2(2, (2, 4))
@@ -378,8 +377,19 @@
             gather(1, b * v)
             gather(2, v * v)
         wrap(v1, 1)
-        for c in range(PIECES):
+        def own_w(c):
             w0[c] = applied(v1, 1, c, 1, (2,))
+
+        for c in from_early:
+            own_w(c)
+
+        @pl.when(early_half)
+        def _():
+            for c in from_early:
+                send_w(c).start()
+
+        for c in from_late:
+            own_w(c)
         each(lambda c: put(v2, 1, c, flat(v2, 1, c) - flat(v1, 1, c)))
         wrap(v2, 1)
         late(1)
@@ -410,7 +420,8 @@
         @pl.when(late_half)
         def _():
             for c in from_early:
-                edge(c)
+                send_w(c).wait_recv()
+                gather(5, -2.0 * flat(v2, 0, c) * (recv_p[c] - flat(v1, 1, c)))
 
     lanes = width // 2
     hi = jnp.zeros((8, lanes), jnp.float32)
@@ -470,8 +481,7 @@
         @pl.when(early_half)
         def _():
             for c in from_early:
-                send_p(c).wait_send()
-                send_r(c).wait_send()
+                send_w(c).wait_send()
 
     sigma, weight = quadrature(SH_DEV * n_shift, tile.shape)
     all_rows(pairs, send_2, got_2).wait_recv()

time: 29.2 us -> 29 us (level)
  no operation moved by 1% of the time
where the time goes in v6:
time: 29 us; the launch traced here: 28.8 us
  Pallas kernels  28 us (97%)
  local copies, waits for them, and re-layouts  0.8 us (3%)
    pallas_call x1, Pallas kernels, on_device(): pl.pallas_call(functools.partial(kernel, n_space, n_shift, column), out_s...  28 us
    unnamed x1, local copies, waits for them, and re-layouts  0.8 us

profile of v6, /device:TPU:1, one launch (start us, length us, event | category | flops | bytes accessed | tf_op | source)
XLA Modules:
  0.0 28.8 jit_solution(5200605901786044358)
XLA Ops:
  0.0 28.0 %shard_map.28 = f32[2,256,256]{2,1,0:T(8,128)S(1)} custom-call(f32[8,256,256]{2,1,0:T(8,128)} %state.1, f32[8,256,256]{2,1,0:T(8,128)} %reaction.1), custom_call_target="tpu_custom_call" | custom-call | flops 13107200 | bytes 5242880 | tf_op jit(solution)/shard_map/pallas_call | solution.py:516
  28.0 0.8 %copy.4 = f32[2,256,256]{2,1,0:T(8,128)} copy(f32[2,256,256]{2,1,0:T(8,128)S(1)} %shard_map.28) | data formatting | bytes 1048576

commit v7 on v6

--- a/solution.py
+++ b/solution.py
@@ -458,12 +458,12 @@
             lost = lost + e
         return merge(total, lost)
 
-    for k in range(len(up)):
-        row_to(tile, tiles, k, send_1, got_1, beside(k)).start()
+    for k in range(len(wide)):
+        row_to(tile, tiles, k, send_1, got_1, across(k)).start()
     all_rows(tiles, send_1, got_1).wait_recv()
     pair[...] = summed(tile[...], tiles)
-    for k in range(len(wide)):
-        row_to(pair, pairs, k, send_2, got_2, across(k)).start()
+    for k in range(len(up)):
+        row_to(pair, pairs, k, send_2, got_2, beside(k)).start()
     all_rows(tiles, send_1, got_1).wait_send()
 
     @pl.when(is_outer)
@@ -532,9 +532,9 @@
             pltpu.VMEM((PIECES, piece, width), f32),
             pltpu.VMEM((6, 8, width), f32),
             pltpu.VMEM((1, width // 2), f32),
+            pltpu.VMEM((columns - 1, 1, width // 2), f32),
+            pltpu.VMEM((1, width // 2), f32),
             pltpu.VMEM((column - 1, 1, width // 2), f32),
-            pltpu.VMEM((1, width // 2), f32),
-            pltpu.VMEM((columns - 1, 1, width // 2), f32),
             dma((7,)),
             dma((5,)),
             dma((4 * PIECES,)),

time: 29 us -> 28.9 us (level)
  no operation moved by 1% of the time
where the time goes in v7:
time: 28.9 us; the launch traced here: 28.8 us
  Pallas kernels  28 us (97%)
  local copies, waits for them, and re-layouts  0.8 us (3%)
    pallas_call x1, Pallas kernels, on_device(): pl.pallas_call(functools.partial(kernel, n_space, n_shift, column), out_s...  28 us
    unnamed x1, local copies, waits for them, and re-layouts  0.8 us

profile of v7, /device:TPU:1, one launch (start us, length us, event | category | flops | bytes accessed | tf_op | source)
XLA Modules:
  0.0 28.8 jit_solution(8304136747578020817)
XLA Ops:
  0.0 28.0 %shard_map.28 = f32[2,256,256]{2,1,0:T(8,128)S(1)} custom-call(f32[8,256,256]{2,1,0:T(8,128)} %state.1, f32[8,256,256]{2,1,0:T(8,128)} %reaction.1), custom_call_target="tpu_custom_call" | custom-call | flops 13107200 | bytes 5242880 | tf_op jit(solution)/shard_map/pallas_call | solution.py:516
  28.0 0.8 %copy.4 = f32[2,256,256]{2,1,0:T(8,128)} copy(f32[2,256,256]{2,1,0:T(8,128)S(1)} %shard_map.28) | data formatting | bytes 1048576
